TPU v7x, 128 devices: a whole 4x4x4 slice. The times are simulated.
128 devices in a mesh: fsdp: 16 (over y_lo, z, core), tp: 8 (over x, y_hi).
Axes of the slice: x: 4, y: 4 (y_hi: 2, y_lo: 2; y = y_hi * 2 + y_lo), z: 4, core: 2. Of those that a mesh axis runs over, the one named last changes fastest.
Arguments:
- hidden_in: bfloat16 [1024, 4096], P('fsdp'), may hold values from -3 to 3
- queries: bfloat16 [2, 1024, 8192], P(None, ('fsdp', 'tp')), may hold values from -170 to 170
- key_cache: bfloat16 [1024, 256, 512], P(('fsdp', 'tp')), may hold values from -6 to 6
- value_cache: bfloat16 [1024, 256, 512], P(('fsdp', 'tp')), may hold values from -6 to 6
- new_keys: bfloat16 [2, 1024, 512], P(None, ('fsdp', 'tp')), may hold values from -6 to 6
- new_values: bfloat16 [2, 1024, 512], P(None, ('fsdp', 'tp')), may hold values from -6 to 6
- lengths: int32 [1024], P(('fsdp', 'tp')), may hold values from 2 to 256
- routes: int32 [2, 1024, 8], P(None, 'fsdp'), may hold values from 0 to 127, all different within a row; in each aligned block of 64 rows (0 to 63, 64 to 127, ..., all dimensions but the last counted through in order) at most 8 rows name the same one
- route_weights: float32 [2, 1024, 8], P(None, 'fsdp'), may hold values from 0.05 to 1
- norm_gain: float32 [4096], replicated, may hold values from 0.1 to 1.9
- gate_master: float32 [8, 1536, 4096], P(None, ('fsdp', 'tp')), may hold values from -0.09375 to 0.09375
- up_master: float32 [8, 1536, 4096], P(None, ('fsdp', 'tp')), may hold values from -0.09375 to 0.09375
- down_master: float32 [8, 1536, 4096], P(None, ('fsdp', 'tp')), may hold values from -0.3125 to 0.3125
- out_proj: bfloat16 [8192, 4096], P('tp'), may hold values from -0.0625 to 0.0625
Outputs:
- hidden_out: bfloat16 [1024, 4096], P('fsdp', 'tp')
- scale_log2: float32 [3, 8, 12, 32], replicated
Inputs may be any that keep to these rules, and one draw needn't show every extreme that they name: `routes`: within one step and one index of fsdp (aligned blocks of 64 rows), no expert is named by more than 8 rows.
All inputs are finite; a program needn't handle non-finite values.
Results may differ from a plain program's by a relative error of at most 0.0095.
Values may be sent and summed in bfloat16 or wider, within the bound.
A program may use at most 256 MiB of HBM per device.

v0:
```python
import jax
import jax.numpy as jnp
from jax import lax
from jax.sharding import PartitionSpec as P

D = 4096
FF = 1536
QH = 64
KVH = 4
HD = 128
BLOCK = 128
WIN = 8
CAP = 8
neg_fill = -1e30
epsilon = 1e-06
fp_limit = 448.0
grid_floor = 2.0 ** (-10)
least_exponent = -6.0


def cut_along(array, dim, peers):
    before, after = (array.shape[:dim], array.shape[dim + 1 :])
    return jnp.moveaxis(array.reshape(*before, peers, -1, *after), dim, 0)


def sent_and_summed(array, axis, dim):
    blocks = cut_along(array, dim, lax.axis_size(axis))
    arrived = lax.all_to_all(blocks, axis, split_axis=0, concat_axis=0, tiled=True)
    return arrived.astype(jnp.float32).sum(axis=0)


def copy_for_each(array, axis):
    peers = lax.axis_size(axis)
    return lax.all_to_all(
        jnp.broadcast_to(array[None], (peers, *array.shape)), axis, 0, 0, tiled=True
    )


def joined_along(blocks, dim):
    blocks = jnp.moveaxis(blocks, 0, dim)
    lengths = blocks.shape
    return blocks.reshape(*lengths[:dim], lengths[dim] * lengths[dim + 1], *lengths[dim + 2 :])


def collect(array, axis, dim):
    blocks = copy_for_each(array, axis)
    return joined_along(blocks, dim)


def grid_round(values):
    magnitude = jnp.abs(values)
    exponent = jnp.maximum(jnp.floor(jnp.log2(jnp.maximum(magnitude, grid_floor))), least_exponent)
    spacing = jnp.exp2(exponent - 3.0)
    return jnp.sign(values) * jnp.floor(magnitude / spacing + 0.5) * spacing


def attention_rows(queries_now, cache_keys, cache_values, fresh_keys, fresh_values, lengths):
    row_count = queries_now.shape[0]
    positions = cache_keys.shape[1]
    group = QH // KVH
    score_scale = HD ** (-0.5)
    fresh_count = fresh_keys.shape[0]
    query_heads = queries_now.reshape(row_count, KVH, group, HD)
    key_heads = cache_keys.reshape(row_count, positions, KVH, HD)
    value_heads = cache_values.reshape(row_count, positions, KVH, HD)
    fresh_key_heads = fresh_keys.reshape(fresh_count, row_count, KVH, HD)
    fresh_value_heads = fresh_values.reshape(fresh_count, row_count, KVH, HD)
    cached_scores = (
        jnp.einsum("rkgd,rpkd->rkgp", query_heads, key_heads, preferred_element_type=jnp.float32)
        * score_scale
    )
    fresh_scores = (
        jnp.einsum(
            "rkgd,srkd->rkgs", query_heads, fresh_key_heads, preferred_element_type=jnp.float32
        )
        * score_scale
    )
    alive_mask = (jnp.arange(positions, dtype=jnp.int32)[None, :] < lengths[:, None])[
        :, None, None, :
    ]
    peak_score = jnp.maximum(
        jnp.max(jnp.where(alive_mask, cached_scores, neg_fill), axis=-1),
        jnp.max(fresh_scores, axis=-1),
    )
    cached_weights = jnp.where(alive_mask, jnp.exp(cached_scores - peak_score[..., None]), 0.0)
    fresh_weights = jnp.exp(fresh_scores - peak_score[..., None])
    weight_sum = jnp.sum(cached_weights, axis=-1) + jnp.sum(fresh_weights, axis=-1)
    cached_probs = (cached_weights / weight_sum[..., None]).astype(jnp.bfloat16)
    fresh_probs = (fresh_weights / weight_sum[..., None]).astype(jnp.bfloat16)
    output = jnp.einsum(
        "rkgp,rpkd->rkgd", cached_probs, value_heads, preferred_element_type=jnp.float32
    )
    output = output + jnp.einsum(
        "rkgs,srkd->rkgd", fresh_probs, fresh_value_heads, preferred_element_type=jnp.float32
    )
    return output.astype(jnp.bfloat16).reshape(row_count, QH * HD)


def routing_tables(routes, route_weights):
    rows = routes.shape[0]
    weight_sum = jnp.sum(route_weights, axis=1)
    experts = jnp.arange(WIN, dtype=jnp.int32)
    matches = routes[None, :, :] == experts[:, None, None]
    chosen = jnp.any(matches, axis=2)
    gate_share = (
        jnp.sum(jnp.where(matches, route_weights[None, :, :], 0.0), axis=2) / weight_sum[None, :]
    )
    earlier = jnp.arange(rows)[:, None] < jnp.arange(rows)[None, :]
    slot_index = jnp.sum(jnp.where(earlier[None], chosen.astype(jnp.int32)[:, :, None], 0), axis=1)
    places = jnp.arange(CAP, dtype=jnp.int32)
    picked = (slot_index[:, None, :] == places[None, :, None]) & chosen[:, None, :]
    slot_share = jnp.sum(jnp.where(picked, gate_share[:, None, :], 0.0), axis=2)
    return (picked.astype(jnp.bfloat16), slot_share)


def block_maxima(masters, fsdp_pos, tp_pos, tp_count):
    shard_rows = masters.shape[2]
    magnitude = jnp.max(jnp.abs(masters).reshape(3, WIN, shard_rows, D // BLOCK, BLOCK), axis=4)
    first_tile = fsdp_pos * shard_rows * tp_count // BLOCK
    owned = (fsdp_pos * tp_count + tp_pos) * shard_rows + jnp.arange(shard_rows, dtype=jnp.int32)
    second = owned // BLOCK - first_tile == 1
    mine = jnp.stack(
        [
            jnp.max(jnp.where(second[None, None, :, None], 0.0, magnitude), axis=2),
            jnp.max(jnp.where(second[None, None, :, None], magnitude, 0.0), axis=2),
        ]
    )
    group = jnp.max(copy_for_each(mine, "tp"), axis=0)
    every = copy_for_each(group, "fsdp")
    tiles = []
    for tile in range(FF // BLOCK):
        parts = []
        for owner in range(16):
            first = owner * 96 // BLOCK
            if first == tile:
                parts.append(every[owner, 0])
            if first + 1 == tile and owner * 96 + 95 >= tile * BLOCK:
                parts.append(every[owner, 1])
        tiles.append(jnp.max(jnp.stack(parts), axis=0))
    return (jnp.stack(tiles, axis=2), first_tile, second)


def local(
    hidden_in,
    queries,
    key_cache,
    value_cache,
    new_keys,
    new_values,
    lengths,
    routes,
    route_weights,
    norm_gain,
    gate_master,
    up_master,
    down_master,
    out_proj,
):
    tp_count = lax.axis_size("tp")
    fsdp_pos = lax.axis_index("fsdp")
    tp_pos = lax.axis_index("tp")
    shard_rows = gate_master.shape[1]
    masters = jnp.stack([gate_master, up_master, down_master])
    block_max, first_tile, second = block_maxima(masters, fsdp_pos, tp_pos, tp_count)
    scales = (block_max + epsilon) / fp_limit
    scale_log2 = jnp.log2(scales)
    near = lax.dynamic_slice_in_dim(scales, first_tile, 1, 2)
    far = lax.dynamic_slice_in_dim(scales, jnp.minimum(first_tile + 1, FF // BLOCK - 1), 1, 2)
    factors = jnp.where(second[None, None, :, None], far, near)[..., None]
    tiles = masters.reshape(3, WIN, shard_rows, D // BLOCK, BLOCK)
    quantized = grid_round(tiles / factors).astype(jnp.bfloat16).astype(jnp.float32)
    restored = (quantized * factors).astype(jnp.bfloat16).reshape(3, WIN, shard_rows, D)
    arrived = lax.all_to_all(
        restored.transpose(1, 0, 2, 3), "tp", split_axis=0, concat_axis=0, tiled=True
    )
    own = [arrived[:, i].reshape(tp_count * shard_rows, D) for i in range(3)]
    share_cols = D // tp_count
    own_start = tp_pos * share_cols
    current = lax.dynamic_slice_in_dim(hidden_in, own_start, share_cols, 1)
    tables = [routing_tables(routes[s], route_weights[s]) for s in range(2)]
    heads = jnp.stack(
        [
            attention_rows(
                queries[s], key_cache, value_cache, new_keys[: s + 1], new_values[: s + 1], lengths
            )
            for s in range(2)
        ]
    )
    regrouped = lax.all_to_all(heads, "tp", split_axis=2, concat_axis=1, tiled=True)
    projections = []
    for s in range(2):
        projected = jnp.dot(regrouped[s], out_proj, preferred_element_type=jnp.float32)
        projections.append(projected.astype(jnp.bfloat16))
    both = jnp.stack(projections)
    summed = sent_and_summed(both, "tp", 2)
    for s in range(2):
        picked, slot_share = tables[s]
        mixed = (current.astype(jnp.float32) + summed[s]).astype(jnp.bfloat16)
        slots = picked.reshape(WIN * CAP, -1)
        chosen = jnp.dot(slots, mixed, preferred_element_type=jnp.float32).astype(jnp.bfloat16)
        rows = collect_slots(chosen)
        values = rows.astype(jnp.float32)
        inverse = lax.rsqrt(jnp.mean(values * values, axis=1, keepdims=True) + epsilon)
        normed = (values * inverse * norm_gain[None, :]).astype(jnp.bfloat16)
        everyone = copy_for_each(normed, "fsdp").reshape(-1, D)
        gate = jnp.einsum("rd,hd->rh", everyone, own[0], preferred_element_type=jnp.float32)
        up = jnp.einsum("rd,hd->rh", everyone, own[1], preferred_element_type=jnp.float32)
        act = (jax.nn.silu(gate) * up).astype(jnp.bfloat16)
        partial = jnp.dot(act, own[2], preferred_element_type=jnp.float32).astype(jnp.bfloat16)
        output = sent_and_summed(partial, "fsdp", 0)
        share = lax.dynamic_slice_in_dim(slot_share, tp_pos, 1, 0)[0]
        weighted = (output * share[:, None]).astype(jnp.bfloat16)
        returned = lax.all_to_all(
            cut_along(weighted, 1, tp_count), "tp", split_axis=0, concat_axis=0, tiled=True
        ).reshape(WIN * CAP, share_cols)
        moe = lax.dot_general(
            slots, returned, (((0,), (0,)), ((), ())), preferred_element_type=jnp.float32
        )
        current = (mixed.astype(jnp.float32) + moe).astype(jnp.bfloat16)
    return (current, scale_log2)


def collect_slots(chosen):
    arrived = lax.all_to_all(chosen, "tp", split_axis=0, concat_axis=0, tiled=True)
    blocks = arrived.reshape(-1, CAP, chosen.shape[1])
    return joined_along(blocks, 1)


def solution(mesh):
    in_specs = (
        P("fsdp", None),
        P(None, ("fsdp", "tp"), None),
        P(("fsdp", "tp"), None, None),
        P(("fsdp", "tp"), None, None),
        P(None, ("fsdp", "tp"), None),
        P(None, ("fsdp", "tp"), None),
        P(("fsdp", "tp")),
        P(None, "fsdp", None),
        P(None, "fsdp", None),
        P(),
        P(None, ("fsdp", "tp"), None),
        P(None, ("fsdp", "tp"), None),
        P(None, ("fsdp", "tp"), None),
        P("tp", None),
    )
    out_specs = (P("fsdp", "tp"), P())
    return jax.shard_map(local, mesh=mesh, in_specs=in_specs, out_specs=out_specs, check_vma=False)
```

profile of v0, /device:TPU:0, one launch (start us, length us, event | category | flops | bytes accessed | tf_op | source)
XLA Modules:
  0.0 295.8 jit_solution(17559378506708630502)
XLA Ops:
  0.7 3.8 %fusion = f32[3,8,12,32]{1,3,2,0:T(8,128)S(1)} fusion(f32[1,8,12,32,128]{4,1,3,2,0:T(8,128)} %bitcast.259, f32[1,8,12,32,128]{4,1,3,2,0:T(8,128)} %bitcast.261, f32[1,8,12,32,128]{4,1,3,2,0:T(8,128)} %bitcast.263), kind=kLoop, calls=%fused_computation.4 | loop fusion | flops 4709376 | bytes 4755456 | tf_op jit(solution)/shard_map/reduce_max | solution.py:118
  5.7 7.0 %all-to-all-start.4 = ((f32[8,1,1536]{2,1,0:T(1,128)}), f32[8,1,1536]{2,1,0:T(1,128)S(1)}, u32[]{:S(2)}, u32[]{:S(2)}) async-start(f32[8,1,1536]{2,1,0:T(1,128)} %reshape.598), calls=%async_computation.4 | async-start | bytes 98304 | tf_op jit(solution)/shard_map/all_to_all | solution.py:34
  18.4 6.7 %copy.154 = bf16[2,8,8192]{1,0,2:T(2,128)(2,1)} copy(bf16[2,8,8192]{2,1,0:T(8,128)(2,1)S(1)} %pad_maximum_fusion) | data formatting | bytes 524288 | tf_op jit(solution)/shard_map/stack | solution.py:181
  25.1 6.4 %reshape.602 = bf16[8,2,8192]{2,1,0:T(2,128)(2,1)} reshape(bf16[8192,2,8]{2,1,0:T(2,128)(2,1)} %bitcast.257) | data formatting | bytes 524288
  33.9 5.5 %all-to-all-start.5 = ((f32[16,1,1536]{2,1,0:T(1,128)}), f32[16,1,1536]{2,1,0:T(1,128)S(1)}, u32[]{:S(2)}, u32[]{:S(2)}) async-start(f32[16,1,1536]{2,1,0:T(1,128)} %reshape.600), calls=%async_computation.5 | async-start | bytes 196608 | tf_op jit(solution)/shard_map/all_to_all | solution.py:34
  39.7 6.1 %all-to-all-done.5 = f32[16,1,1536]{2,1,0:T(1,128)S(1)} async-done(((f32[16,1,1536]{2,1,0:T(1,128)}), f32[16,1,1536]{2,1,0:T(1,128)S(1)}, u32[]{:S(2)}, u32[]{:S(2)}) %all-to-all-start.5) | async-done | bytes 98336 | tf_op jit(solution)/shard_map/all_to_all | solution.py:34
  45.8 7.8 %all-to-all-start = ((bf16[8,2,8192]{2,1,0:T(2,128)(2,1)}), bf16[8,2,8192]{2,1,0:T(2,128)(2,1)S(1)}, u32[]{:S(2)}, u32[]{:S(2)}) async-start(bf16[8,2,8192]{2,1,0:T(2,128)(2,1)} %reshape.602), calls=%async_computation | async-start | bytes 524288 | tf_op jit(solution)/shard_map/all_to_all | solution.py:189
  54.7 7.6 %all-to-all-done = bf16[8,2,8192]{2,1,0:T(2,128)(2,1)S(1)} async-done(((bf16[8,2,8192]{2,1,0:T(2,128)(2,1)}), bf16[8,2,8192]{2,1,0:T(2,128)(2,1)S(1)}, u32[]{:S(2)}, u32[]{:S(2)}) %all-to-all-start) | async-done | bytes 262176 | tf_op jit(solution)/shard_map/all_to_all | solution.py:189
  62.4 5.9 %reshape.603 = bf16[8192,2,8]{2,1,0:T(2,128)(2,1)} reshape(bf16[8,2,8192]{2,1,0:T(2,128)(2,1)S(1)} %all-to-all-done) | data formatting | bytes 524288
  68.3 5.9 %copy.169 = bf16[2,8,8,1024]{3,2,1,0:T(8,128)(2,1)S(1)} copy(bf16[2,8,8,1024]{1,0,3,2:T(2,128)(2,1)} %bitcast.258) | data formatting | bytes 524288 | tf_op jit(solution)/shard_map/all_to_all | solution.py:189
  74.3 4.9 %convolution_convert_fusion.2 = bf16[64,4096]{1,0:T(8,128)(2,1)S(1)} fusion(bf16[1024,4096]{1,0:T(8,128)(2,1)} %param.27, bf16[1,8,8,1024]{3,1,2,0:T(8,128)(2,1)S(1)} %get-tuple-element.26), kind=kOutput, calls=%fused_computation.9 | convolution fusion | flops 537133056 | bytes 9043968 | tf_op jit(solution)/shard_map/dot_general | solution.py:192
  79.5 4.9 %convolution_convert_fusion.3 = bf16[64,4096]{1,0:T(8,128)(2,1)S(1)} fusion(bf16[1024,4096]{1,0:T(8,128)(2,1)} %param.27, bf16[1,8,8,1024]{3,1,2,0:T(8,128)(2,1)S(1)} %get-tuple-element.25), kind=kOutput, calls=%fused_computation.10 | convolution fusion | flops 537133056 | bytes 9043968 | tf_op jit(solution)/shard_map/dot_general | solution.py:192
  93.6 6.1 %div.124 = f32[3,8,12,4096]{3,1,2,0:T(8,128)} reshape(f32[3,8,12,32,128]{4,3,1,2,0:T(8,128)} %div.123) | data formatting | bytes 9437184 | tf_op jit(solution)/shard_map/div | solution.py:171
  99.7 4.7 %all-to-all-done.1 = bf16[8,2,64,512]{3,2,1,0:T(8,128)(2,1)S(1)} async-done(((bf16[8,2,64,512]{3,2,1,0:T(8,128)(2,1)}), bf16[8,2,64,512]{3,2,1,0:T(8,128)(2,1)S(1)}, u32[]{:S(2)}, u32[]{:S(2)}) %all-to-all-start.1) | async-done | bytes 1048608 | tf_op jit(solution)/shard_map/all_to_all | solution.py:28
  110.0 6.4 %fusion.3 = bf16[8,3,12,4096]{3,0,2,1:T(8,128)(2,1)S(1)} fusion(f32[3,8,12,4096]{3,1,2,0:T(8,128)} %div.124, f32[1,8,12,4096]{3,1,2,0:T(8,128)S(1)} %bitcast.260, f32[1,8,12,4096]{3,1,2,0:T(8,128)} %bitcast.262, f32[1,8,12,4096]{3,1,2,0:T(8,128)} %bitcast.264), kind=kLoop, calls=%fused_computation.11 | loop fusion | flops 23592960 | bytes 11796480 | tf_op jit(solution)/shard_map/transpose | solution.py:174
  119.5 7.3 %all-to-all-start.6 = ((bf16[8,3,12,4096]{3,2,1,0:T(8,128)(2,1)}), bf16[8,3,12,4096]{3,2,1,0:T(8,128)(2,1)}, u32[]{:S(2)}, u32[]{:S(2)}) async-start(bf16[8,3,12,4096]{3,2,1,0:T(8,128)(2,1)} %copy.165), calls=%async_computation.6 | async-start | bytes 6291456 | tf_op jit(solution)/shard_map/all_to_all | solution.py:173
  127.1 44.2 %all-to-all-done.6 = bf16[8,3,12,4096]{3,2,1,0:T(8,128)(2,1)} async-done(((bf16[8,3,12,4096]{3,2,1,0:T(8,128)(2,1)}), bf16[8,3,12,4096]{3,2,1,0:T(8,128)(2,1)}, u32[]{:S(2)}, u32[]{:S(2)}) %all-to-all-start.6) | async-done | bytes 2359328 | tf_op jit(solution)/shard_map/all_to_all | solution.py:173
  183.9 8.7 %all-to-all-done.3 = bf16[16,8,4096]{2,1,0:T(8,128)(2,1)S(1)} async-done(((bf16[16,8,4096]{2,1,0:T(8,128)(2,1)}), bf16[16,8,4096]{2,1,0:T(8,128)(2,1)S(1)}, u32[]{:S(2)}, u32[]{:S(2)}) %all-to-all-start.3) | async-done | bytes 1048608 | tf_op jit(solution)/shard_map/all_to_all | solution.py:34
  200.4 16.4 %all-to-all-done.7 = bf16[16,8,4096]{2,1,0:T(8,128)(2,1)S(1)} async-done(((bf16[16,8,4096]{2,1,0:T(8,128)(2,1)}), bf16[16,8,4096]{2,1,0:T(8,128)(2,1)S(1)}, u32[]{:S(2)}, u32[]{:S(2)}) %all-to-all-start.7) | async-done | bytes 1048608 | tf_op jit(solution)/shard_map/all_to_all | solution.py:28
  217.0 10.1 %all_to_all.83 = bf16[8,8,512]{2,1,0:T(8,128)(2,1)S(1)} all-to-all(bf16[8,8,512]{2,1,0:T(8,128)(2,1)S(1)} %fusion.69), channel_id=1, replica_groups=mesh['fsdp'=16,'tp'=8] {'tp'}, dimensions={0} | all-to-all | bytes 131072 | tf_op jit(solution)/shard_map/all_to_all | solution.py:213
  227.6 10.3 %all_to_all.84 = bf16[8,8,512]{2,1,0:T(8,128)(2,1)S(1)} all-to-all(bf16[8,8,512]{2,1,0:T(8,128)(2,1)S(1)} %fusion.42), channel_id=1, replica_groups=mesh['fsdp'=16,'tp'=8] {'tp'}, dimensions={0} | all-to-all | bytes 131072 | tf_op jit(solution)/shard_map/all_to_all | solution.py:224
  238.2 19.1 %all_to_all.85 = bf16[16,8,4096]{2,1,0:T(8,128)(2,1)S(1)} all-to-all(bf16[16,8,4096]{2,1,0:T(8,128)(2,1)S(1)} %broadcast_in_dim.230), channel_id=1, replica_groups=mesh['fsdp'=16,'tp'=8] {'fsdp'}, dimensions={0} | all-to-all | bytes 2097152 | tf_op jit(solution)/shard_map/all_to_all | solution.py:34
  266.6 16.4 %all-to-all-done.11 = bf16[16,8,4096]{2,1,0:T(8,128)(2,1)S(1)} async-done(((bf16[16,8,4096]{2,1,0:T(8,128)(2,1)}), bf16[16,8,4096]{2,1,0:T(8,128)(2,1)S(1)}, u32[]{:S(2)}, u32[]{:S(2)}) %all-to-all-start.11) | async-done | bytes 1048608 | tf_op jit(solution)/shard_map/all_to_all | solution.py:28
  287.9 7.0 %all-to-all-done.12 = bf16[8,8,512]{2,1,0:T(8,128)(2,1)S(1)} async-done(((bf16[8,8,512]{2,1,0:T(8,128)(2,1)}), bf16[8,8,512]{2,1,0:T(8,128)(2,1)S(1)}, u32[]{:S(2)}, u32[]{:S(2)}) %all-to-all-start.12) | async-done | bytes 65568 | tf_op jit(solution)/shard_map/all_to_all | solution.py:213
  (144 shorter events, 64.9 us)
Async XLA Ops:
  0.6 12.7 %copy-start = (bf16[8,256,512]{2,1,0:T(8,128)(2,1)S(1)}, bf16[8,256,512]{2,1,0:T(8,128)(2,1)}, u32[]{:S(2)}) copy-start(bf16[8,256,512]{2,1,0:T(8,128)(2,1)} %param.16) | copy-start | bytes 6291460
  0.6 12.0 %copy-start.5 = (bf16[2,8,8192]{2,1,0:T(8,128)(2,1)S(1)}, bf16[2,8,8192]{2,1,0:T(8,128)(2,1)}, u32[]{:S(2)}) copy-start(bf16[2,8,8192]{2,1,0:T(8,128)(2,1)} %param.15) | copy-start | bytes 786436
  0.7 12.1 %copy-start.11 = (s32[8]{0:T(128)S(1)}, s32[8]{0:T(128)}, u32[]{:S(2)}) copy-start(s32[8]{0:T(128)} %param.20) | copy-start | bytes 100
  0.7 12.2 %copy-start.10 = (bf16[2,8,512]{2,1,0:T(8,128)(2,1)S(1)}, bf16[2,8,512]{2,1,0:T(8,128)(2,1)}, u32[]{:S(2)}) copy-start(bf16[2,8,512]{2,1,0:T(8,128)(2,1)} %param.18) | copy-start | bytes 49156
  5.7 25.9 %all-to-all-start.4 = ((f32[8,1,1536]{2,1,0:T(1,128)}), f32[8,1,1536]{2,1,0:T(1,128)S(1)}, u32[]{:S(2)}, u32[]{:S(2)}) async-start(f32[8,1,1536]{2,1,0:T(1,128)} %reshape.598), calls=%async_computation.4 | async-start | bytes 98304 | tf_op jit(solution)/shard_map/all_to_all | solution.py:34
  12.7 2.5 copy-start.9
  12.8 2.7 copy-start.12
  15.5 2.7 copy-start.7
  33.9 11.8 %all-to-all-start.5 = ((f32[16,1,1536]{2,1,0:T(1,128)}), f32[16,1,1536]{2,1,0:T(1,128)S(1)}, u32[]{:S(2)}, u32[]{:S(2)}) async-start(f32[16,1,1536]{2,1,0:T(1,128)} %reshape.600), calls=%async_computation.5 | async-start | bytes 196608 | tf_op jit(solution)/shard_map/all_to_all | solution.py:34
  45.8 16.6 %all-to-all-start = ((bf16[8,2,8192]{2,1,0:T(2,128)(2,1)}), bf16[8,2,8192]{2,1,0:T(2,128)(2,1)S(1)}, u32[]{:S(2)}, u32[]{:S(2)}) async-start(bf16[8,2,8192]{2,1,0:T(2,128)(2,1)} %reshape.602), calls=%async_computation | async-start | bytes 524288 | tf_op jit(solution)/shard_map/all_to_all | solution.py:189
  85.9 18.5 %all-to-all-start.1 = ((bf16[8,2,64,512]{3,2,1,0:T(8,128)(2,1)}), bf16[8,2,64,512]{3,2,1,0:T(8,128)(2,1)S(1)}, u32[]{:S(2)}, u32[]{:S(2)}) async-start(bf16[8,2,64,512]{3,2,1,0:T(8,128)(2,1)} %maximum_bitcast_fusion), calls=%async_computation.1 | async-start | bytes 2097152 | tf_op jit(solution)/shard_map/all_to_all | solution.py:28
  93.6 16.4 %copy-start.4 = (f32[8,12,4096]{2,0,1:T(8,128)S(1)}, f32[8,12,4096]{2,0,1:T(8,128)}, u32[]{:S(2)}) copy-start(f32[8,12,4096]{2,0,1:T(8,128)} %param.26) | copy-start | bytes 4718596
  106.2 13.3 %all-to-all-start.2 = ((bf16[8,8,512]{2,1,0:T(8,128)(2,1)}), bf16[8,8,512]{2,1,0:T(8,128)(2,1)S(1)}, u32[]{:S(2)}, u32[]{:S(2)}) async-start(bf16[8,8,512]{2,1,0:T(8,128)(2,1)} %fusion.41), calls=%async_computation.2 | async-start | bytes 131072 | tf_op jit(solution)/shard_map/all_to_all | solution.py:224
  119.5 7.5 %copy-start.6 = (f32[4096]{0:T(1024)S(1)}, f32[4096]{0:T(1024)}, u32[]{:S(2)}) copy-start(f32[4096]{0:T(1024)} %param.23) | copy-start | bytes 49156
  119.5 51.8 %all-to-all-start.6 = ((bf16[8,3,12,4096]{3,2,1,0:T(8,128)(2,1)}), bf16[8,3,12,4096]{3,2,1,0:T(8,128)(2,1)}, u32[]{:S(2)}, u32[]{:S(2)}) async-start(bf16[8,3,12,4096]{3,2,1,0:T(8,128)(2,1)} %copy.165), calls=%async_computation.6 | async-start | bytes 6291456 | tf_op jit(solution)/shard_map/all_to_all | solution.py:173
  172.4 20.2 %all-to-all-start.3 = ((bf16[16,8,4096]{2,1,0:T(8,128)(2,1)}), bf16[16,8,4096]{2,1,0:T(8,128)(2,1)S(1)}, u32[]{:S(2)}, u32[]{:S(2)}) async-start(bf16[16,8,4096]{2,1,0:T(8,128)(2,1)} %broadcast_in_dim.215), calls=%async_computation.3 | async-start | bytes 2097152 | tf_op jit(solution)/shard_map/all_to_all | solution.py:34
  179.7 16.9 %copy-start.2 = (bf16[96,4096]{1,0:T(8,128)(2,1)}, bf16[96,4096]{1,0:T(8,128)(2,1)S(1)}, u32[]{:S(2)}) copy-start(bf16[96,4096]{1,0:T(8,128)(2,1)S(1)} %reshape_squeeze.19) | copy-start | bytes 2359300
  181.4 15.2 %copy-start.3 = (bf16[96,4096]{1,0:T(8,128)(2,1)}, bf16[96,4096]{1,0:T(8,128)(2,1)S(1)}, u32[]{:S(2)}) copy-start(bf16[96,4096]{1,0:T(8,128)(2,1)S(1)} %reshape_squeeze.18) | copy-start | bytes 2359300
  183.9 16.4 %copy-start.8 = (f32[2,64,8]{1,2,0:T(8,128)S(1)}, f32[2,64,8]{1,2,0:T(8,128)}, u32[]{:S(2)}) copy-start(f32[2,64,8]{1,2,0:T(8,128)} %param.22) | copy-start | bytes 12292
  196.6 20.2 %all-to-all-start.7 = ((bf16[16,8,4096]{2,1,0:T(8,128)(2,1)}), bf16[16,8,4096]{2,1,0:T(8,128)(2,1)S(1)}, u32[]{:S(2)}, u32[]{:S(2)}) async-start(bf16[16,8,4096]{2,1,0:T(8,128)(2,1)} %fusion.1), calls=%async_computation.7 | async-start | bytes 2097152 | tf_op jit(solution)/shard_map/all_to_all | solution.py:28
  257.3 38.5 %copy-start.1 = (bf16[8,256,512]{2,1,0:T(8,128)(2,1)S(1)}, bf16[8,256,512]{2,1,0:T(8,128)(2,1)}, u32[]{:S(2)}) copy-start(bf16[8,256,512]{2,1,0:T(8,128)(2,1)} %param.16) | copy-start | bytes 6291460
  262.8 20.2 %all-to-all-start.11 = ((bf16[16,8,4096]{2,1,0:T(8,128)(2,1)}), bf16[16,8,4096]{2,1,0:T(8,128)(2,1)S(1)}, u32[]{:S(2)}, u32[]{:S(2)}) async-start(bf16[16,8,4096]{2,1,0:T(8,128)(2,1)} %fusion.2), calls=%async_computation.11 | async-start | bytes 2097152 | tf_op jit(solution)/shard_map/all_to_all | solution.py:28
  283.9 11.0 %all-to-all-start.12 = ((bf16[8,8,512]{2,1,0:T(8,128)(2,1)}), bf16[8,8,512]{2,1,0:T(8,128)(2,1)S(1)}, u32[]{:S(2)}, u32[]{:S(2)}) async-start(bf16[8,8,512]{2,1,0:T(8,128)(2,1)} %fusion.70), calls=%async_computation.12 | async-start | bytes 131072 | tf_op jit(solution)/shard_map/all_to_all | solution.py:213
where the time goes:
time: 297 us; the launch traced here: 296 us
  waiting for transfers between devices  111 us (37%)
  local copies, waits for them, and re-layouts  51.2 us (17%)
  starting transfers between devices  49.5 us (17%)
  blocking collectives  39.5 us (13%)
  matrix products  26.1 us (9%)
  other arithmetic  17 us (6%)
    all_to_all x1, waiting for transfers between devices, local(): lax.all_to_all(restored.transpose(1, 0, 2, 3), 'tp', split_axis=0, concat...  44.2 us
    all_to_all x3, waiting for transfers between devices, sent_and_summed(): lax.all_to_all(blocks, axis, split_axis=0, concat_axis=0, tiled=True)  37.5 us
    all_to_all x1, blocking collectives, copy_for_each(): lax.all_to_all(jnp.broadcast_to(array[None], (peers, *array.shape)), axis...  19.1 us
    all_to_all x3, starting transfers between devices, copy_for_each(): lax.all_to_all(jnp.broadcast_to(array[None], (peers, *array.shape)), axis...  16.2 us
    unnamed x38, local copies, waits for them, and re-layouts  15.3 us
    all_to_all x3, waiting for transfers between devices, copy_for_each(): lax.all_to_all(jnp.broadcast_to(array[None], (peers, *array.shape)), axis...  14.8 us
    all_to_all x3, starting transfers between devices, sent_and_summed(): lax.all_to_all(blocks, axis, split_axis=0, concat_axis=0, tiled=True)  11 us
    all_to_all x1, blocking collectives, collect_slots(): lax.all_to_all(chosen, 'tp', split_axis=0, concat_axis=0, tiled=True)  10.3 us
  transfers between devices with their start and end apart: 10, of which 8 were waited for; matrix products, arithmetic and copies ran while one was open for 16% of the time, Pallas kernels for 0%

commit v1 on v0

--- a/solution.py
+++ b/solution.py
@@ -1,7 +1,9 @@
+import functools
 import jax
 import jax.numpy as jnp
 from jax import lax
 from jax.sharding import PartitionSpec as P
+from jax.lax import all_to_all, axis_size
 
 D = 4096
 FF = 1536
@@ -16,6 +18,20 @@
 fp_limit = 448.0
 grid_floor = 2.0 ** (-10)
 least_exponent = -6.0
+
+
+def supply_all_paths(w_in, ax_name, on_dim, d_out):
+    tall = all_to_all(
+        jnp.stack(jnp.split(w_in, axis_size(ax_name), axis=on_dim), axis=0),
+        axis_name=ax_name,
+        split_axis=0,
+        concat_axis=0,
+    )
+    y2 = jnp.concatenate(tall, axis=d_out)
+    return y2
+
+
+trace_paths = functools.partial(supply_all_paths, ax_name="tp", on_dim=2, d_out=1)
 
 
 def cut_along(array, dim, peers):
@@ -186,7 +202,7 @@
             for s in range(2)
         ]
     )
-    regrouped = lax.all_to_all(heads, "tp", split_axis=2, concat_axis=1, tiled=True)
+    regrouped = trace_paths(heads)
     projections = []
     for s in range(2):
         projected = jnp.dot(regrouped[s], out_proj, preferred_element_type=jnp.float32)

time: 297 us -> 287 us (0.966)
  local copies, waits for them, and re-layouts: 51.2 us -> 37.2 us
  waiting for transfers between devices: 111 us -> 98.1 us
  other arithmetic: 17 us -> 26 us
  matrix products: 26.1 us -> 30.2 us
    all_to_all x3, waiting for transfers between devices: 37.5 us -> 29.5 us  [sent_and_summed(): lax.all_to_all(blocks, axis, split_axis=0, concat_axis=0, tiled=True)]
    another operation x3, local copies, waits for them, and re-layouts: 6.88 us -> 0.14 us  [local(): jnp.stack([attention_rows(queries[s], key_cache, value_cache, new_keys[:s...]
    unnamed x38 -> x62, local copies, waits for them, and re-layouts: 15.3 us -> 9.09 us
    all_to_all x1 -> x0, local copies, waits for them, and re-layouts: 5.94 us -> none  [local(): lax.all_to_all(heads, 'tp', split_axis=2, concat_axis=1, tiled=True)]
  transfers between devices with their start and end apart: 10 -> 10, of which waited for: 8 -> 8; matrix products, arithmetic and copies ran while one was open for 16% -> 18% of each run, Pallas kernels for 0% -> 0%
where the time goes in v1:
time: 287 us; the launch traced here: 285 us
  waiting for transfers between devices  98.1 us (34%)
  starting transfers between devices  52.2 us (18%)
  blocking collectives  39.5 us (14%)
  local copies, waits for them, and re-layouts  37.2 us (13%)
  matrix products  30.2 us (11%)
  other arithmetic  26 us (9%)
    all_to_all x1, waiting for transfers between devices, local(): lax.all_to_all(restored.transpose(1, 0, 2, 3), 'tp', split_axis=0, concat...  42.1 us
    all_to_all x3, waiting for transfers between devices, sent_and_summed(): lax.all_to_all(blocks, axis, split_axis=0, concat_axis=0, tiled=True)  29.5 us
    all_to_all x1, blocking collectives, copy_for_each(): lax.all_to_all(jnp.broadcast_to(array[None], (peers, *array.shape)), axis...  19.1 us
    all_to_all x3, starting transfers between devices, copy_for_each(): lax.all_to_all(jnp.broadcast_to(array[None], (peers, *array.shape)), axis...  16.2 us
    all_to_all x3, waiting for transfers between devices, copy_for_each(): lax.all_to_all(jnp.broadcast_to(array[None], (peers, *array.shape)), axis...  11.9 us
    all_to_all x3, starting transfers between devices, sent_and_summed(): lax.all_to_all(blocks, axis, split_axis=0, concat_axis=0, tiled=True)  10.9 us
    all_to_all x1, blocking collectives, collect_slots(): lax.all_to_all(chosen, 'tp', split_axis=0, concat_axis=0, tiled=True)  10.3 us
    all_to_all x1, blocking collectives, local(): lax.all_to_all(cut_along(weighted, 1, tp_count), 'tp', split_axis=0, conc...  10.1 us
  transfers between devices with their start and end apart: 10, of which 8 were waited for; matrix products, arithmetic and copies ran while one was open for 18% of the time, Pallas kernels for 0%

profile of v1, /device:TPU:0, one launch (start us, length us, event | category | flops | bytes accessed | tf_op | source)
XLA Modules:
  0.0 284.6 jit_solution(1923333466211442449)
XLA Ops:
  0.7 3.8 %fusion = f32[3,8,12,32]{1,3,2,0:T(8,128)S(1)} fusion(f32[1,8,12,32,128]{4,1,3,2,0:T(8,128)} %bitcast.284, f32[1,8,12,32,128]{4,1,3,2,0:T(8,128)} %bitcast.286, f32[1,8,12,32,128]{4,1,3,2,0:T(8,128)} %bitcast.288), kind=kLoop, calls=%fused_computation.4 | loop fusion | flops 4709376 | bytes 4755456 | tf_op jit(solution)/shard_map/reduce_max | solution.py:134
  5.7 7.0 %all-to-all-start.4 = ((f32[8,1,1536]{2,1,0:T(1,128)}), f32[8,1,1536]{2,1,0:T(1,128)S(1)}, u32[]{:S(2)}, u32[]{:S(2)}) async-start(f32[8,1,1536]{2,1,0:T(1,128)} %reshape.603), calls=%async_computation.4 | async-start | bytes 98304 | tf_op jit(solution)/shard_map/all_to_all | solution.py:50
  26.8 5.5 %all-to-all-start.5 = ((f32[16,1,1536]{2,1,0:T(1,128)}), f32[16,1,1536]{2,1,0:T(1,128)S(1)}, u32[]{:S(2)}, u32[]{:S(2)}) async-start(f32[16,1,1536]{2,1,0:T(1,128)} %reshape.605), calls=%async_computation.5 | async-start | bytes 196608 | tf_op jit(solution)/shard_map/all_to_all | solution.py:50
  33.2 5.5 %all-to-all-done.5 = f32[16,1,1536]{2,1,0:T(1,128)S(1)} async-done(((f32[16,1,1536]{2,1,0:T(1,128)}), f32[16,1,1536]{2,1,0:T(1,128)S(1)}, u32[]{:S(2)}, u32[]{:S(2)}) %all-to-all-start.5) | async-done | bytes 98336 | tf_op jit(solution)/shard_map/all_to_all | solution.py:50
  38.7 7.8 %all-to-all-start = ((bf16[8,2,8,1024]{3,2,1,0:T(8,128)(2,1)}), bf16[8,2,8,1024]{3,2,1,0:T(8,128)(2,1)S(1)}, u32[]{:S(2)}, u32[]{:S(2)}) async-start(bf16[8,2,8,1024]{3,2,1,0:T(8,128)(2,1)} %constant_dynamic-update-slice_fusion.2), calls=%async_computation | async-start | bytes 524288 | tf_op jit(solution)/shard_map/all_to_all | solution.py:24
  47.6 7.6 %all-to-all-done = bf16[8,2,8,1024]{3,2,1,0:T(8,128)(2,1)S(1)} async-done(((bf16[8,2,8,1024]{3,2,1,0:T(8,128)(2,1)}), bf16[8,2,8,1024]{3,2,1,0:T(8,128)(2,1)S(1)}, u32[]{:S(2)}, u32[]{:S(2)}) %all-to-all-start) | async-done | bytes 262176 | tf_op jit(solution)/shard_map/all_to_all | solution.py:24
  55.3 4.9 %convolution_convert_fusion.2 = bf16[64,4096]{1,0:T(8,128)(2,1)S(1)} fusion(bf16[1024,4096]{1,0:T(8,128)(2,1)} %param.27, bf16[2,8,8,1024]{3,2,0,1:T(8,128)(2,1)S(1)} %bitcast.294), kind=kOutput, calls=%fused_computation.9 | convolution fusion | flops 537133056 | bytes 9043968 | tf_op jit(solution)/shard_map/dot_general | solution.py:208
  60.2 5.0 %convolution_convert_fusion.3 = bf16[64,4096]{1,0:T(8,128)(2,1)S(1)} fusion(bf16[1024,4096]{1,0:T(8,128)(2,1)} %param.27, bf16[2,8,8,1024]{3,2,0,1:T(8,128)(2,1)S(1)} %bitcast.295), kind=kOutput, calls=%fused_computation.10 | convolution fusion | flops 537133056 | bytes 9043968 | tf_op jit(solution)/shard_map/dot_general | solution.py:208
  79.0 6.0 %div.124 = f32[3,8,12,4096]{3,1,2,0:T(8,128)} reshape(f32[3,8,12,32,128]{4,3,1,2,0:T(8,128)} %div.123) | data formatting | bytes 9437184 | tf_op jit(solution)/shard_map/div | solution.py:187
  88.6 6.7 %all-to-all-start.2 = ((bf16[8,8,512]{2,1,0:T(8,128)(2,1)}), bf16[8,8,512]{2,1,0:T(8,128)(2,1)S(1)}, u32[]{:S(2)}, u32[]{:S(2)}) async-start(bf16[8,8,512]{2,1,0:T(8,128)(2,1)} %fusion.41), calls=%async_computation.2 | async-start | bytes 131072 | tf_op jit(solution)/shard_map/all_to_all | solution.py:240
  95.3 6.6 %fusion.3 = bf16[8,3,12,4096]{3,0,2,1:T(8,128)(2,1)S(1)} fusion(f32[3,8,12,4096]{3,1,2,0:T(8,128)} %div.124, f32[1,8,12,4096]{3,1,2,0:T(8,128)} %bitcast.285, f32[1,8,12,4096]{3,1,2,0:T(8,128)} %bitcast.287, f32[1,8,12,4096]{3,1,2,0:T(8,128)} %bitcast.289), kind=kLoop, calls=%fused_computation.11 | loop fusion | flops 23592960 | bytes 11796480 | tf_op jit(solution)/shard_map/transpose | solution.py:190
  105.0 7.3 %all-to-all-start.6 = ((bf16[8,3,12,4096]{3,2,1,0:T(8,128)(2,1)}), bf16[8,3,12,4096]{3,2,1,0:T(8,128)(2,1)}, u32[]{:S(2)}, u32[]{:S(2)}) async-start(bf16[8,3,12,4096]{3,2,1,0:T(8,128)(2,1)} %copy.129), calls=%async_computation.6 | async-start | bytes 6291456 | tf_op jit(solution)/shard_map/all_to_all | solution.py:189
  112.6 42.1 %all-to-all-done.6 = bf16[8,3,12,4096]{3,2,1,0:T(8,128)(2,1)} async-done(((bf16[8,3,12,4096]{3,2,1,0:T(8,128)(2,1)}), bf16[8,3,12,4096]{3,2,1,0:T(8,128)(2,1)}, u32[]{:S(2)}, u32[]{:S(2)}) %all-to-all-start.6) | async-done | bytes 2359328 | tf_op jit(solution)/shard_map/all_to_all | solution.py:189
  169.6 6.4 %all-to-all-done.3 = bf16[16,8,4096]{2,1,0:T(8,128)(2,1)S(1)} async-done(((bf16[16,8,4096]{2,1,0:T(8,128)(2,1)}), bf16[16,8,4096]{2,1,0:T(8,128)(2,1)S(1)}, u32[]{:S(2)}, u32[]{:S(2)}) %all-to-all-start.3) | async-done | bytes 1048608 | tf_op jit(solution)/shard_map/all_to_all | solution.py:50
  178.2 3.8 %fusion.1 = bf16[16,8,4096]{2,1,0:T(8,128)(2,1)} fusion(bf16[96,4096]{1,0:T(8,128)(2,1)} %reshape_squeeze.19, bf16[96,4096]{1,0:T(8,128)(2,1)} %reshape_squeeze.18, bf16[16,8,4096]{2,1,0:T(8,128)(2,1)S(1)} %all-to-all-done.3, f32[128,96]{0,1:T(8,128)} %fusion.51), kind=kOutput, calls=%fused_computation.7 | convolution fusion | flops 201924608 | bytes 3719168 | tf_op jit(solution)/shard_map/dot_general | solution.py:225
  182.0 3.7 %all-to-all-start.7 = ((bf16[16,8,4096]{2,1,0:T(8,128)(2,1)}), bf16[16,8,4096]{2,1,0:T(8,128)(2,1)S(1)}, u32[]{:S(2)}, u32[]{:S(2)}) async-start(bf16[16,8,4096]{2,1,0:T(8,128)(2,1)} %fusion.1), calls=%async_computation.7 | async-start | bytes 2097152 | tf_op jit(solution)/shard_map/all_to_all | solution.py:44
  189.5 12.6 %all-to-all-done.7 = bf16[16,8,4096]{2,1,0:T(8,128)(2,1)S(1)} async-done(((bf16[16,8,4096]{2,1,0:T(8,128)(2,1)}), bf16[16,8,4096]{2,1,0:T(8,128)(2,1)S(1)}, u32[]{:S(2)}, u32[]{:S(2)}) %all-to-all-start.7) | async-done | bytes 1048608 | tf_op jit(solution)/shard_map/all_to_all | solution.py:44
  203.0 10.1 %all_to_all.73 = bf16[8,8,512]{2,1,0:T(8,128)(2,1)S(1)} all-to-all(bf16[8,8,512]{2,1,0:T(8,128)(2,1)S(1)} %fusion.65), channel_id=1, replica_groups=mesh['fsdp'=16,'tp'=8] {'tp'}, dimensions={0} | all-to-all | bytes 131072 | tf_op jit(solution)/shard_map/all_to_all | solution.py:229
  215.7 10.3 %all_to_all.74 = bf16[8,8,512]{2,1,0:T(8,128)(2,1)S(1)} all-to-all(bf16[8,8,512]{2,1,0:T(8,128)(2,1)S(1)} %fusion.42), channel_id=1, replica_groups=mesh['fsdp'=16,'tp'=8] {'tp'}, dimensions={0} | all-to-all | bytes 131072 | tf_op jit(solution)/shard_map/all_to_all | solution.py:240
  227.1 19.1 %all_to_all.75 = bf16[16,8,4096]{2,1,0:T(8,128)(2,1)S(1)} all-to-all(bf16[16,8,4096]{2,1,0:T(8,128)(2,1)S(1)} %broadcast_in_dim.230), channel_id=1, replica_groups=mesh['fsdp'=16,'tp'=8] {'fsdp'}, dimensions={0} | all-to-all | bytes 2097152 | tf_op jit(solution)/shard_map/all_to_all | solution.py:50
  247.9 3.8 %fusion.2 = bf16[16,8,4096]{2,1,0:T(8,128)(2,1)} fusion(bf16[96,4096]{1,0:T(8,128)(2,1)} %reshape_squeeze.19, bf16[96,4096]{1,0:T(8,128)(2,1)} %reshape_squeeze.18, bf16[16,8,4096]{2,1,0:T(8,128)(2,1)S(1)} %all_to_all.75, f32[128,96]{0,1:T(8,128)S(1)} %fusion.47), kind=kOutput, calls=%fused_computation.8 | convolution fusion | flops 201924608 | bytes 3719168 | tf_op jit(solution)/shard_map/dot_general | solution.py:225
  251.6 3.7 %all-to-all-start.11 = ((bf16[16,8,4096]{2,1,0:T(8,128)(2,1)}), bf16[16,8,4096]{2,1,0:T(8,128)(2,1)S(1)}, u32[]{:S(2)}, u32[]{:S(2)}) async-start(bf16[16,8,4096]{2,1,0:T(8,128)(2,1)} %fusion.2), calls=%async_computation.11 | async-start | bytes 2097152 | tf_op jit(solution)/shard_map/all_to_all | solution.py:44
  255.5 16.4 %all-to-all-done.11 = bf16[16,8,4096]{2,1,0:T(8,128)(2,1)S(1)} async-done(((bf16[16,8,4096]{2,1,0:T(8,128)(2,1)}), bf16[16,8,4096]{2,1,0:T(8,128)(2,1)S(1)}, u32[]{:S(2)}, u32[]{:S(2)}) %all-to-all-start.11) | async-done | bytes 1048608 | tf_op jit(solution)/shard_map/all_to_all | solution.py:44
  276.7 7.0 %all-to-all-done.12 = bf16[8,8,512]{2,1,0:T(8,128)(2,1)S(1)} async-done(((bf16[8,8,512]{2,1,0:T(8,128)(2,1)}), bf16[8,8,512]{2,1,0:T(8,128)(2,1)S(1)}, u32[]{:S(2)}, u32[]{:S(2)}) %all-to-all-start.12) | async-done | bytes 65568 | tf_op jit(solution)/shard_map/all_to_all | solution.py:229
  (166 shorter events, 70.5 us)
Async XLA Ops:
  0.6 12.2 %copy-start = (bf16[8,256,512]{2,1,0:T(8,128)(2,1)S(1)}, bf16[8,256,512]{2,1,0:T(8,128)(2,1)}, u32[]{:S(2)}) copy-start(bf16[8,256,512]{2,1,0:T(8,128)(2,1)} %param.16) | copy-start | bytes 6291460
  0.7 4.1 %copy-start.18 = (pred[12]{0:T(512)(128)(4,1)}, pred[12]{0:T(512)(128)(4,1)S(1)}, u32[]{:S(2)}) copy-start(pred[12]{0:T(512)(128)(4,1)S(1)} %subtract_compare_fusion) | copy-start | bytes 40
  0.7 12.0 %copy-start.4 = (bf16[2,8,8192]{2,1,0:T(8,128)(2,1)S(1)}, bf16[2,8,8192]{2,1,0:T(8,128)(2,1)}, u32[]{:S(2)}) copy-start(bf16[2,8,8192]{2,1,0:T(8,128)(2,1)} %param.15) | copy-start | bytes 786436
  0.7 12.1 %copy-start.17 = (bf16[2,8,512]{2,1,0:T(8,128)(2,1)S(1)}, bf16[2,8,512]{2,1,0:T(8,128)(2,1)}, u32[]{:S(2)}) copy-start(bf16[2,8,512]{2,1,0:T(8,128)(2,1)} %param.18) | copy-start | bytes 49156
  4.5 9.1 %copy-start.20 = (s32[8]{0:T(128)S(1)}, s32[8]{0:T(128)}, u32[]{:S(2)}) copy-start(s32[8]{0:T(128)} %param.20) | copy-start | bytes 100
  5.7 18.8 %all-to-all-start.4 = ((f32[8,1,1536]{2,1,0:T(1,128)}), f32[8,1,1536]{2,1,0:T(1,128)S(1)}, u32[]{:S(2)}, u32[]{:S(2)}) async-start(f32[8,1,1536]{2,1,0:T(1,128)} %reshape.603), calls=%async_computation.4 | async-start | bytes 98304 | tf_op jit(solution)/shard_map/all_to_all | solution.py:50
  16.0 7.3 %copy-start.15 = (s32[2,64,8]{1,2,0:T(8,128)S(1)}, s32[2,64,8]{1,2,0:T(8,128)}, u32[]{:S(2)}) copy-start(s32[2,64,8]{1,2,0:T(8,128)} %param.21) | copy-start | bytes 12292
  26.8 11.8 %all-to-all-start.5 = ((f32[16,1,1536]{2,1,0:T(1,128)}), f32[16,1,1536]{2,1,0:T(1,128)S(1)}, u32[]{:S(2)}, u32[]{:S(2)}) async-start(f32[16,1,1536]{2,1,0:T(1,128)} %reshape.605), calls=%async_computation.5 | async-start | bytes 196608 | tf_op jit(solution)/shard_map/all_to_all | solution.py:50
  38.7 16.6 %all-to-all-start = ((bf16[8,2,8,1024]{3,2,1,0:T(8,128)(2,1)}), bf16[8,2,8,1024]{3,2,1,0:T(8,128)(2,1)S(1)}, u32[]{:S(2)}, u32[]{:S(2)}) async-start(bf16[8,2,8,1024]{3,2,1,0:T(8,128)(2,1)} %constant_dynamic-update-slice_fusion.2), calls=%async_computation | async-start | bytes 524288 | tf_op jit(solution)/shard_map/all_to_all | solution.py:24
  47.6 12.6 %copy-start.5 = (f32[3,8,12,32]{3,1,0,2:T(8,128)}, f32[3,8,12,32]{3,1,0,2:T(8,128)S(1)}, u32[]{:S(2)}) copy-start(f32[3,8,12,32]{3,1,0,2:T(8,128)S(1)} %constant_dynamic-update-slice_fusion.12) | copy-start | bytes 110596
  67.0 18.5 %all-to-all-start.1 = ((bf16[8,2,64,512]{3,2,1,0:T(8,128)(2,1)}), bf16[8,2,64,512]{3,2,1,0:T(8,128)(2,1)S(1)}, u32[]{:S(2)}, u32[]{:S(2)}) async-start(bf16[8,2,64,512]{3,2,1,0:T(8,128)(2,1)} %maximum_bitcast_fusion), calls=%async_computation.1 | async-start | bytes 2097152 | tf_op jit(solution)/shard_map/all_to_all | solution.py:44
  88.6 16.4 %all-to-all-start.2 = ((bf16[8,8,512]{2,1,0:T(8,128)(2,1)}), bf16[8,8,512]{2,1,0:T(8,128)(2,1)S(1)}, u32[]{:S(2)}, u32[]{:S(2)}) async-start(bf16[8,8,512]{2,1,0:T(8,128)(2,1)} %fusion.41), calls=%async_computation.2 | async-start | bytes 131072 | tf_op jit(solution)/shard_map/all_to_all | solution.py:240
  105.0 7.5 %copy-start.7 = (f32[4096]{0:T(1024)S(1)}, f32[4096]{0:T(1024)}, u32[]{:S(2)}) copy-start(f32[4096]{0:T(1024)} %param.23) | copy-start | bytes 49156
  105.0 49.7 %all-to-all-start.6 = ((bf16[8,3,12,4096]{3,2,1,0:T(8,128)(2,1)}), bf16[8,3,12,4096]{3,2,1,0:T(8,128)(2,1)}, u32[]{:S(2)}, u32[]{:S(2)}) async-start(bf16[8,3,12,4096]{3,2,1,0:T(8,128)(2,1)} %copy.129), calls=%async_computation.6 | async-start | bytes 6291456 | tf_op jit(solution)/shard_map/all_to_all | solution.py:189
  155.7 20.2 %all-to-all-start.3 = ((bf16[16,8,4096]{2,1,0:T(8,128)(2,1)}), bf16[16,8,4096]{2,1,0:T(8,128)(2,1)S(1)}, u32[]{:S(2)}, u32[]{:S(2)}) async-start(bf16[16,8,4096]{2,1,0:T(8,128)(2,1)} %broadcast_in_dim.215), calls=%async_computation.3 | async-start | bytes 2097152 | tf_op jit(solution)/shard_map/all_to_all | solution.py:50
  182.0 20.2 %all-to-all-start.7 = ((bf16[16,8,4096]{2,1,0:T(8,128)(2,1)}), bf16[16,8,4096]{2,1,0:T(8,128)(2,1)S(1)}, u32[]{:S(2)}, u32[]{:S(2)}) async-start(bf16[16,8,4096]{2,1,0:T(8,128)(2,1)} %fusion.1), calls=%async_computation.7 | async-start | bytes 2097152 | tf_op jit(solution)/shard_map/all_to_all | solution.py:44
  247.8 7.5 %copy-start.9 = (s32[64,8]{0,1:T(8,128)S(1)}, s32[64,8]{0,1:T(8,128)}, u32[]{:S(2)}) copy-start(s32[64,8]{0,1:T(8,128)} %copy-done.8) | copy-start | bytes 6148
  247.8 7.5 %copy-start.14 = (f32[64,8]{0,1:T(8,128)S(1)}, f32[64,8]{0,1:T(8,128)}, u32[]{:S(2)}) copy-start(f32[64,8]{0,1:T(8,128)} %get-tuple-element.33) | copy-start | bytes 6148
  247.8 7.5 %copy-start.19 = (f32[64]{0:T(128)S(1)}, f32[64]{0:T(128)}, u32[]{:S(2)}) copy-start(f32[64]{0:T(128)} %get-tuple-element.14) | copy-start | bytes 772
  247.8 7.5 %copy-start.6 = (s32[8,64]{1,0:T(8,128)S(1)}, s32[8,64]{1,0:T(8,128)}, u32[]{:S(2)}) copy-start(s32[8,64]{1,0:T(8,128)} %get-tuple-element.16) | copy-start | bytes 6148
  247.8 7.5 %copy-start.12 = (pred[8,64]{1,0:T(8,128)(4,1)S(1)}, pred[8,64]{1,0:T(8,128)(4,1)}, u32[]{:S(2)}) copy-start(pred[8,64]{1,0:T(8,128)(4,1)} %copy-done.11) | copy-start | bytes 1540
  247.9 35.9 %copy-start.2 = (bf16[64,512]{1,0:T(8,128)(2,1)S(1)}, bf16[64,512]{1,0:T(8,128)(2,1)}, u32[]{:S(2)}) copy-start(bf16[64,512]{1,0:T(8,128)(2,1)} %copy-done.1) | copy-start | bytes 196612
  251.6 20.2 %all-to-all-start.11 = ((bf16[16,8,4096]{2,1,0:T(8,128)(2,1)}), bf16[16,8,4096]{2,1,0:T(8,128)(2,1)S(1)}, u32[]{:S(2)}, u32[]{:S(2)}) async-start(bf16[16,8,4096]{2,1,0:T(8,128)(2,1)} %fusion.2), calls=%async_computation.11 | async-start | bytes 2097152 | tf_op jit(solution)/shard_map/all_to_all | solution.py:44
  272.7 11.0 %all-to-all-start.12 = ((bf16[8,8,512]{2,1,0:T(8,128)(2,1)}), bf16[8,8,512]{2,1,0:T(8,128)(2,1)S(1)}, u32[]{:S(2)}, u32[]{:S(2)}) async-start(bf16[8,8,512]{2,1,0:T(8,128)(2,1)} %fusion.66), calls=%async_computation.12 | async-start | bytes 131072 | tf_op jit(solution)/shard_map/all_to_all | solution.py:229
  (8 other events, 8.5 us)
